TPU v7x, 256 devices: a whole 4x4x8 slice. The times are simulated.
256 devices in a mesh: rep: 32 (over y, x, core), fsdp: 8 (over z).
Axes of the slice: x: 4, y: 4, z: 8, core: 2. Of those that a mesh axis runs over, the one named last changes fastest.
Arguments:
- codes: bfloat16 [32, 4096, 1024], P('rep', 'fsdp'), may hold values from -127 to 127
- block_scales: float32 [32, 4096, 8], P('rep', 'fsdp'), may hold values from 0.002 to 0.02
- params: bfloat16 [4096, 1024], P('fsdp'), may hold values from -6 to 6
- momentum: bfloat16 [4096, 1024], P('fsdp'), may hold values from -3 to 3
Outputs:
- new_params: bfloat16 [4096, 1024], replicated
- new_momentum: bfloat16 [4096, 1024], P('fsdp')
All inputs are finite; a program needn't handle non-finite values.
Results may differ from a plain program's by a relative error of at most 0.006.
Values may be sent and summed in bfloat16 or wider, within the bound.
A program may use at most 64 MiB of HBM per device.

v0:
```python
import jax
import jax.numpy as jnp
from jax import lax
from jax.sharding import Mesh
from jax.sharding import PartitionSpec as P

REP = ("rep_0", "rep_1", "rep_2")


def filled_up(lines, peers):
    spare = -len(lines) % peers
    return jnp.pad(lines, [(0, spare)] + [(0, 0)] * (lines.ndim - 1))


def sent_to_all(shard, axis):
    copies = jnp.broadcast_to(shard, (lax.axis_size(axis), *shard.shape))
    return lax.all_to_all(copies, axis, split_axis=0, concat_axis=0, tiled=True)


def joined_along(blocks, dim):
    blocks = jnp.moveaxis(blocks, 0, dim)
    lengths = blocks.shape
    return blocks.reshape(*lengths[:dim], lengths[dim] * lengths[dim + 1], *lengths[dim + 2 :])


def whole_of(shard, axes, dim):
    far, near = axes
    first = sent_to_all(shard, far)
    blocks = jnp.swapaxes(sent_to_all(first, near), 0, 1)
    return joined_along(blocks.reshape(-1, *shard.shape), dim)


def in_blocks(shard, dim, peers):
    before, after = (shard.shape[:dim], shard.shape[dim + 1 :])
    return jnp.moveaxis(shard.reshape(*before, peers, -1, *after), dim, 0)


def sum_at_owner(shard, axis, dim):
    blocks = in_blocks(shard, dim, lax.axis_size(axis))
    arrived = lax.all_to_all(blocks, axis, split_axis=0, concat_axis=0, tiled=True)
    return arrived.astype(jnp.float32).sum(axis=0)


def summed_rows(shard, axes, dim):
    far, near = axes
    own = sum_at_owner(in_blocks(shard, dim, lax.axis_size(far)), near, dim + 1)
    return jnp.sum(
        lax.all_to_all(own.astype(jnp.bfloat16), far, 0, 0, tiled=True).astype(jnp.float32), axis=0
    )


def sum_by_parts(shard, axes):
    lines = shard.reshape(-1, shard.shape[-1])
    padded = filled_up(lines, lax.axis_size(axes[0]) * lax.axis_size(axes[1]))
    whole = whole_of(summed_rows(padded, axes, 0).astype(jnp.bfloat16), axes, 0)
    return lax.slice_in_dim(whole, 0, len(lines)).reshape(shard.shape).astype(jnp.float32)


def dequantize(code_rows, scale_rows):
    count, width = code_rows.shape
    pieces = (
        code_rows.astype(jnp.float32).reshape(count, width // 128, 128) * scale_rows[:, :, None]
    )
    return pieces.reshape(count, width)


def outer_update(total, params, momentum, replicas):
    delta = total / replicas
    moment = 0.9 * momentum.astype(jnp.float32) + delta
    updated = (params.astype(jnp.float32) - 0.7 * (delta + 0.9 * moment)).astype(jnp.bfloat16)
    return (updated, moment.astype(jnp.bfloat16))


def local(codes, block_scales, params, momentum):
    replicas = lax.axis_size(REP)
    local_term = dequantize(codes[0], block_scales[0])
    total = sum_by_parts(local_term.astype(jnp.bfloat16), (("rep_0", "rep_1"), "rep_2"))
    updated, new_momentum = outer_update(total, params, momentum, replicas)
    new_params = lax.all_gather(updated, "fsdp", axis=0, tiled=True)
    return (new_params, new_momentum)


def solution(mesh):
    finer = Mesh(
        mesh.devices.reshape(4, 4, 2, mesh.shape["fsdp"]), ("rep_0", "rep_1", "rep_2", "fsdp")
    )
    placed = (P(REP, "fsdp", None), P(REP, "fsdp", None), P("fsdp", None), P("fsdp", None))
    return jax.shard_map(
        local, mesh=finer, in_specs=placed, out_specs=(P(), P("fsdp", None)), check_vma=False
    )
```

profile of v0, /device:TPU:1, one launch (start us, length us, event | category | flops | bytes accessed | tf_op | source)
XLA Modules:
  0.0 167.0 jit_solution(15279222004547587232)
XLA Ops:
  7.2 0.0 all-gather.2.cloned.1.call-start
  7.2 0.8 copy.11
  8.1 0.6 mul.27
  8.7 0.0 copy-start
  8.7 1.5 mul.28
  10.2 0.0 copy-done
  10.2 1.9 %fusion.5 = bf16[2,16,16,1024]{3,2,0,1:T(8,128)(2,1)S(1)} fusion(f32[16,2,16,1024]{3,2,1,0:T(8,128)} %mul.28, bf16[16,2,16,1024]{3,2,1,0:T(8,128)(2,1)S(1)} %bitcast.20), kind=kLoop, calls=%fused_computation.9 | loop fusion | flops 1572864 | bytes 4194304 | tf_op jit(solution)/shard_map/transpose | solution.py:35
  12.1 0.1 copy.12
  12.2 7.4 %all_to_all.20 = bf16[2,16,16,1024]{3,2,1,0:T(8,128)(2,1)S(1)} all-to-all(bf16[2,16,16,1024]{3,2,1,0:T(8,128)(2,1)S(1)} %copy.12), channel_id=1, replica_groups=mesh['rep_0'=4,'rep_1'=4,'rep_2'=2,'fsdp'=8] {'rep_2'}, dimensions={0} | all-to-all | bytes 2097152 | tf_op jit(solution)/shard_map/all_to_all | solution.py:40
  19.6 0.3 reduce_sum.24
  19.9 15.5 %all_to_all.21 = bf16[16,16,1024]{2,1,0:T(8,128)(2,1)S(1)} all-to-all(bf16[16,16,1024]{2,1,0:T(8,128)(2,1)S(1)} %reduce_sum.24), channel_id=1, replica_groups=mesh['rep_0'=4,'rep_1'=4,'rep_2'=2,'fsdp'=8] {'rep_0','rep_1'}, dimensions={0} | all-to-all | bytes 1048576 | tf_op jit(solution)/shard_map/all_to_all | solution.py:48
  35.4 0.1 reduce_sum.25
  35.5 0.1 broadcast_in_dim.6
  35.6 13.4 %all_to_all.22 = bf16[16,16,1024]{2,1,0:T(8,128)(2,1)S(1)} all-to-all(bf16[16,16,1024]{2,1,0:T(8,128)(2,1)S(1)} %broadcast_in_dim.6), channel_id=1, replica_groups=mesh['rep_0'=4,'rep_1'=4,'rep_2'=2,'fsdp'=8] {'rep_0','rep_1'}, dimensions={0} | all-to-all | bytes 1048576 | tf_op jit(solution)/shard_map/all_to_all | solution.py:17
  49.0 0.1 broadcast_in_dim.7
  49.1 6.5 %all_to_all.23 = bf16[2,16,16,1024]{3,2,1,0:T(8,128)(2,1)S(1)} all-to-all(bf16[2,16,16,1024]{3,2,1,0:T(8,128)(2,1)S(1)} %broadcast_in_dim.7), channel_id=1, replica_groups=mesh['rep_0'=4,'rep_1'=4,'rep_2'=2,'fsdp'=8] {'rep_2'}, dimensions={0} | all-to-all | bytes 2097152 | tf_op jit(solution)/shard_map/all_to_all | solution.py:17
  55.7 0.0 copy-start.1
  55.7 0.0 copy-start.2
  55.7 0.3 convert_multiply_fusion.1
  55.9 1.0 copy-done.1
  56.9 0.3 copy-done.2
  57.2 2.0 %fusion.4 = (bf16[512,1024]{1,0:T(8,128)(2,1)}, bf16[512,1024]{1,0:T(8,128)(2,1)}) fusion(f32[2,16,16,1024]{3,2,0,1:T(8,128)S(1)} %convert_multiply_fusion.1, bf16[512,1024]{1,0:T(8,128)(2,1)S(1)} %copy-done.1, bf16[512,1024]{1,0:T(8,128)(2,1)S(1)} %copy-done.2), kind=kLoop, calls=%fused_computation.7 | loop fusion | flops 5242880 | bytes 6291456 | tf_op jit(solution)/shard_map/convert_element_type | solution.py:71
  59.3 0.0 all-gather.2.cloned.1.call-update
  59.3 93.1 %all-gather.2.cloned.1.call-done = bf16[4096,1024]{1,0:T(8,128)(2,1)} async-done(((bf16[512,1024]{1,0:T(8,128)(2,1)}), bf16[4096,1024]{1,0:T(8,128)(2,1)}) %all-gather.2.cloned.1.call-update) | async-done | bytes 8388624 | tf_op jit(solution)/shard_map/all_gather | solution.py:79
  152.4 7.8 %copy.16 = bf16[4096,1024]{1,0:T(8,128)(2,1)} copy(bf16[4096,1024]{1,0:T(8,128)(2,1)} %all-gather.2.cloned.1.call-done) | data formatting | bytes 16777216
Async XLA Ops:
  7.2 145.2 %all-gather.2.cloned.1.call-start = ((), (), s32[]{:S(2)}) async-start(), calls=%async_computation.4 | async-start | bytes 9437184 | tf_op jit(solution)/shard_map/all_gather | solution.py:79
  8.7 1.5 copy-start
  55.7 1.2 copy-start.1
  55.7 1.5 copy-start.2
Sparse Core Ops, SparseCore 0:
  59.4 92.9 all-gather.1
where the time goes:
time: 167 us
  waiting for transfers between devices  93.1 us (56%)
  blocking collectives  42.9 us (26%)
  between operations  14.1 us (8%)
  local copies, waits for them, and re-layouts  12.2 us (7%)
  other arithmetic  4.57 us (3%)
    all_gather x1, waiting for transfers between devices, local(): new_params = lax.all_gather(updated, 'fsdp', axis=0, tiled=True)  93.1 us
    all_to_all x2, blocking collectives, sent_to_all(): return lax.all_to_all(copies, axis, split_axis=0, concat_axis=0, tiled=True)  20 us
    all_to_all x1, blocking collectives, summed_rows(): lax.all_to_all(own.astype(jnp.bfloat16), far, 0, 0, tiled=True)  15.5 us
    unnamed x7, local copies, waits for them, and re-layouts  9.05 us
    all_to_all x1, blocking collectives, sum_at_owner(): lax.all_to_all(blocks, axis, split_axis=0, concat_axis=0, tiled=True)  7.44 us
  transfers between devices with their start and end apart: 1, of which 1 were waited for; matrix products, arithmetic and copies ran while one was open for 0% of the time, Pallas kernels for 0%

commit v1 on v0

--- a/solution.py
+++ b/solution.py
@@ -5,6 +5,11 @@
 from jax.sharding import PartitionSpec as P
 
 REP = ("rep_0", "rep_1", "rep_2")
+
+
+def gather_by_exchange(x, axis, dim):
+    copies = jnp.concatenate([x] * lax.axis_size(axis), axis=dim)
+    return lax.all_to_all(copies, axis, dim, dim, tiled=True)
 
 
 def filled_up(lines, peers):
@@ -76,7 +81,7 @@
     local_term = dequantize(codes[0], block_scales[0])
     total = sum_by_parts(local_term.astype(jnp.bfloat16), (("rep_0", "rep_1"), "rep_2"))
     updated, new_momentum = outer_update(total, params, momentum, replicas)
-    new_params = lax.all_gather(updated, "fsdp", axis=0, tiled=True)
+    new_params = gather_by_exchange(updated, "fsdp", 0)
     return (new_params, new_momentum)
 
 

time: 167 us -> 254 us (1.52)
  blocking collectives: 42.9 us -> 237 us
  waiting for transfers between devices: 93.1 us -> 0 us
  between operations: 14.1 us -> 0.77 us
    all_to_all x0 -> x1, blocking collectives: none -> 193 us  [gather_by_exchange(): return lax.all_to_all(copies, axis, dim, dim, tiled=True)]
    all_gather x1 -> x0, waiting for transfers between devices: 93.1 us -> none  [local(): new_params = lax.all_gather(updated, 'fsdp', axis=0, tiled=True)]
    unnamed x7 -> x12, local copies, waits for them, and re-layouts: 9.05 us -> 8.26 us
  transfers between devices with their start and end apart: 1 -> 0, of which waited for: 1 -> 0; matrix products, arithmetic and copies ran while one was open for 0% -> 0% of each run, Pallas kernels for 0% -> 0%
where the time goes in v1:
time: 254 us; the launch traced here: 253 us
  blocking collectives  237 us (93%)
  local copies, waits for them, and re-layouts  11.5 us (5%)
  other arithmetic  4.49 us (2%)
    all_to_all x1, blocking collectives, gather_by_exchange(): return lax.all_to_all(copies, axis, dim, dim, tiled=True)  193 us
    all_to_all x2, blocking collectives, sent_to_all(): return lax.all_to_all(copies, axis, split_axis=0, concat_axis=0, tiled=True)  20.1 us
    all_to_all x1, blocking collectives, summed_rows(): lax.all_to_all(own.astype(jnp.bfloat16), far, 0, 0, tiled=True)  15.5 us
    unnamed x12, local copies, waits for them, and re-layouts  8.26 us
    all_to_all x1, blocking collectives, sum_at_owner(): lax.all_to_all(blocks, axis, split_axis=0, concat_axis=0, tiled=True)  7.57 us

profile of v1, /device:TPU:1, one launch (start us, length us, event | category | flops | bytes accessed | tf_op | source)
XLA Modules:
  0.0 253.3 jit_solution(172869467467009527)
XLA Ops:
  0.6 0.8 copy.11
  1.5 0.6 mul.27
  2.1 1.5 mul.28
  3.6 2.2 fusion.5
  5.8 0.0 copy-start
  5.8 0.1 copy.12
  5.9 7.6 %all_to_all.32 = bf16[2,16,16,1024]{3,2,1,0:T(8,128)(2,1)S(1)} all-to-all(bf16[2,16,16,1024]{3,2,1,0:T(8,128)(2,1)S(1)} %copy.12), channel_id=1, replica_groups=mesh['rep_0'=4,'rep_1'=4,'rep_2'=2,'fsdp'=8] {'rep_2'}, dimensions={0} | all-to-all | bytes 2097152 | tf_op jit(solution)/shard_map/all_to_all | solution.py:45
  13.4 0.3 reduce_sum.24
  13.7 15.5 %all_to_all.33 = bf16[16,16,1024]{2,1,0:T(8,128)(2,1)S(1)} all-to-all(bf16[16,16,1024]{2,1,0:T(8,128)(2,1)S(1)} %reduce_sum.24), channel_id=1, replica_groups=mesh['rep_0'=4,'rep_1'=4,'rep_2'=2,'fsdp'=8] {'rep_0','rep_1'}, dimensions={0} | all-to-all | bytes 1048576 | tf_op jit(solution)/shard_map/all_to_all | solution.py:53
  29.2 0.0 copy-start.1
  29.2 0.1 reduce_sum.25
  29.3 0.1 broadcast_in_dim.6
  29.4 13.6 %all_to_all.34 = bf16[16,16,1024]{2,1,0:T(8,128)(2,1)S(1)} all-to-all(bf16[16,16,1024]{2,1,0:T(8,128)(2,1)S(1)} %broadcast_in_dim.6), channel_id=1, replica_groups=mesh['rep_0'=4,'rep_1'=4,'rep_2'=2,'fsdp'=8] {'rep_0','rep_1'}, dimensions={0} | all-to-all | bytes 1048576 | tf_op jit(solution)/shard_map/all_to_all | solution.py:22
  42.9 0.1 broadcast_in_dim.7
  43.1 6.5 %all_to_all.35 = bf16[2,16,16,1024]{3,2,1,0:T(8,128)(2,1)S(1)} all-to-all(bf16[2,16,16,1024]{3,2,1,0:T(8,128)(2,1)S(1)} %broadcast_in_dim.7), channel_id=1, replica_groups=mesh['rep_0'=4,'rep_1'=4,'rep_2'=2,'fsdp'=8] {'rep_2'}, dimensions={0} | all-to-all | bytes 2097152 | tf_op jit(solution)/shard_map/all_to_all | solution.py:22
  49.6 0.3 convert_multiply_fusion.1
  49.9 0.0 copy-done
  49.9 0.0 copy-done.1
  49.9 1.7 fusion.4
  51.6 0.1 constant_dynamic-update-slice_fusion.7
  51.7 0.1 constant_dynamic-update-slice_fusion.6
  51.7 0.1 constant_dynamic-update-slice_fusion.5
  51.8 0.1 constant_dynamic-update-slice_fusion.4
  51.9 0.1 constant_dynamic-update-slice_fusion.3
  52.0 0.1 constant_dynamic-update-slice_fusion.2
  52.1 0.1 constant_dynamic-update-slice_fusion.1
  52.1 0.1 constant_dynamic-update-slice_fusion
  52.2 193.3 %all_to_all.36 = bf16[8,512,1024]{2,1,0:T(8,128)(2,1)} all-to-all(bf16[8,512,1024]{2,1,0:T(8,128)(2,1)S(1)} %bitcast.23), channel_id=1, replica_groups=mesh['rep_0'=4,'rep_1'=4,'rep_2'=2,'fsdp'=8] {'fsdp'}, dimensions={0} | all-to-all | bytes 16777216 | tf_op jit(solution)/shard_map/all_to_all | solution.py:12
  245.5 7.8 %copy.23 = bf16[4096,1024]{1,0:T(8,128)(2,1)} copy(bf16[4096,1024]{1,0:T(8,128)(2,1)} %bitcast.22) | data formatting | bytes 16777216
Async XLA Ops:
  5.8 44.1 %copy-start = (bf16[512,1024]{1,0:T(8,128)(2,1)S(1)}, bf16[512,1024]{1,0:T(8,128)(2,1)}, u32[]{:S(2)}) copy-start(bf16[512,1024]{1,0:T(8,128)(2,1)} %param.7) | copy-start | bytes 3145732
  29.2 20.6 %copy-start.1 = (bf16[512,1024]{1,0:T(8,128)(2,1)S(1)}, bf16[512,1024]{1,0:T(8,128)(2,1)}, u32[]{:S(2)}) copy-start(bf16[512,1024]{1,0:T(8,128)(2,1)} %param.6) | copy-start | bytes 3145732
